TPU v7x, 32 devices: a whole 2x2x4 slice. The times are simulated.
32 devices in a mesh: gx: 8 (over z, core), gy: 4 (over y, x).
Axes of the slice: x: 2, y: 2, z: 4, core: 2. Of those that a mesh axis runs over, the one named last changes fastest.
Arguments:
- member_flows: float32 [24, 4, 64, 32, 128], P(None, None, 'gx', 'gy'), may hold values from -6 to 6
- wall_texture: float32 [24, 64, 32], P(None, 'gx', 'gy'), may hold values from 0.2 to 2
- cross_link_matrix: float32 [4, 4], replicated, may hold values from -3 to 3
- obs_owner: int32 [4, 4096], replicated, may hold values from 0 to 31
- obs_cell: int32 [4, 4096], replicated, may hold values from 0 to 8191
- obs_value: float32 [4, 4096], replicated, may hold values from -8 to 8
- obs_var: float32 [4, 4096], replicated, may hold values from 0.1 to 1
- local_mask: int32 [4, 8, 4, 64], P(None, 'gx', 'gy'), may hold values 0 or 1
Outputs:
- analysis: float32 [24, 4, 64, 32, 128], P(None, None, 'gx', 'gy')
- rough_post: float32 [24, 64, 32], P(None, 'gx', 'gy')
Inputs may be any that keep to these rules, and one draw needn't show every extreme that they name: `obs_owner`: observations are skewed towards a few tiles.
All inputs are finite; a program needn't handle non-finite values. No bound on the sum of `local_mask` on one device may be relied on, other than what follows from the above.
Results may differ from a plain program's by a relative error of at most 0.0003.
Values sent between devices are 32-bit elements; how exact they have to be, the bound alone decides.
A program may use at most 64 MiB of HBM per device.

v0:
```python
import jax
import jax.numpy as jnp
from jax import lax
from jax.sharding import PartitionSpec as P

BATCHES = 4
OBS_BLOCK = 64


def padded_2(block, sides, width):
    for axis, dim in sides:
        count = lax.axis_size(axis)
        forward = [(i, i + 1) for i in range(count - 1)]
        backward = [(target, source) for source, target in forward]
        low = lax.ppermute(
            lax.slice_in_dim(block, block.shape[dim] - width, None, axis=dim), axis, forward
        )
        high = lax.ppermute(lax.slice_in_dim(block, 0, width, axis=dim), axis, backward)
        block = jnp.concatenate([low, block, high], axis=dim)
    return block


def prior_flow_vector(member_flow_vector, wall_texture_entries, cross_link_matrix):
    padded = padded_2(member_flow_vector, (("gx", 2), ("gy", 3)), 1)
    padded = jnp.pad(padded, ((0, 0), (0, 0), (0, 0), (0, 0), (1, 1)))
    center = padded[:, :, 1:-1, 1:-1, 1:-1]
    lap = padded[:, :, 2:, 1:-1, 1:-1] + padded[:, :, :-2, 1:-1, 1:-1]
    lap = lap + padded[:, :, 1:-1, 2:, 1:-1] + padded[:, :, 1:-1, :-2, 1:-1]
    lap = lap + padded[:, :, 1:-1, 1:-1, 2:] + padded[:, :, 1:-1, 1:-1, :-2] - 6.0 * center
    slope = 0.5 * (padded[:, :, 2:, 1:-1, 1:-1] - padded[:, :, :-2, 1:-1, 1:-1])
    mixed = jnp.einsum(
        "fg,mgxyz->mfxyz", cross_link_matrix, center, precision=lax.Precision.HIGHEST
    )
    level = (lax.broadcasted_iota(jnp.int32, (center.shape[-1],), 0) == 0).astype(jnp.float32)
    drag = wall_texture_entries[:, None, :, :, None] * center * level
    return center + 0.5 * (0.15 * lap - 0.6 * slope + mixed - drag)


def observation_terms(values, value_b, var_b):
    members = values.shape[0]
    ybar = jnp.mean(values, axis=0)
    dev = values - ybar[None, :]
    spread = jnp.sum(dev * dev, axis=0) / (members - 1.0)
    root = jnp.sqrt(spread + var_b)
    gterm = ((value_b - ybar) / (spread + var_b))[None, :] - dev / (
        root * (jnp.sqrt(var_b) + root)
    )[None, :]
    return (dev, gterm)


def apply_mixing(member_flow_vector, wall_texture_entries, mixing):
    flat_state = member_flow_vector.reshape(member_flow_vector.shape[0], -1)
    prime = flat_state - jnp.mean(flat_state, axis=0, keepdims=True)
    member_flow_vector = (
        flat_state + jnp.dot(mixing.T, prime, precision=lax.Precision.HIGHEST)
    ).reshape(member_flow_vector.shape)
    flat_rough = wall_texture_entries.reshape(wall_texture_entries.shape[0], -1)
    rprime = flat_rough - jnp.mean(flat_rough, axis=0, keepdims=True)
    wall_texture_entries = (
        flat_rough + jnp.dot(mixing.T, rprime, precision=lax.Precision.HIGHEST)
    ).reshape(wall_texture_entries.shape)
    return (member_flow_vector, wall_texture_entries)


def on_device(
    member_flows,
    wall_texture,
    cross_link_matrix,
    obs_owner,
    obs_cell,
    obs_value,
    obs_var,
    local_mask,
):
    members = member_flows.shape[0]
    cells = member_flows.shape[2] * member_flows.shape[3] * member_flows.shape[4]
    member_flow_vector = prior_flow_vector(member_flows, wall_texture, cross_link_matrix)
    wall_texture_entries = wall_texture
    mytile = lax.axis_index("gx") * lax.axis_size("gy") + lax.axis_index("gy")
    for batch in range(BATCHES):
        flat_first = member_flow_vector[:, 0].reshape(members, cells)
        picked = jnp.take(flat_first, obs_cell[batch], axis=1)
        owned = (obs_owner[batch] == mytile)[None, :]
        local_vals = jnp.where(owned, picked, 0.0)
        block_weight = local_mask[batch, 0, 0].astype(jnp.float32)
        values = lax.psum(local_vals, ("gx", "gy"))
        dev, gterm = observation_terms(values, obs_value[batch], obs_var[batch])
        weighted = dev * jnp.repeat(block_weight, OBS_BLOCK)[None, :]
        mixing = jnp.dot(weighted, gterm.T, precision=lax.Precision.HIGHEST) / (members - 1.0)
        member_flow_vector, wall_texture_entries = apply_mixing(
            member_flow_vector, wall_texture_entries, mixing
        )
    return (member_flow_vector, wall_texture_entries)


def solution(mesh):
    return jax.shard_map(
        on_device,
        mesh=mesh,
        in_specs=(
            P(None, None, "gx", "gy", None),
            P(None, "gx", "gy"),
            P(),
            P(),
            P(),
            P(),
            P(),
            P(None, "gx", "gy", None),
        ),
        out_specs=(P(None, None, "gx", "gy", None), P(None, "gx", "gy")),
        check_vma=False,
    )
```

profile of v0, /device:TPU:0, one launch (start us, length us, event | category | flops | bytes accessed | tf_op | source)
XLA Modules:
  0.0 787.5 jit_solution(4160225619469467906)
XLA Ops:
  7.3 4.5 copy.87
  14.4 3.1 collective-permute-start.1
  22.1 2.7 constant_dynamic-update-slice_fusion.1
  29.2 4.9 collective-permute-start.3
  37.4 4.0 collective-permute-done.2
  43.1 9.1 %select_maximum_fusion = f32[24,4,10,10,130]{4,1,3,2,0:T(4,128)S(1)} fusion(f32[24,4,10,1,128]{4,1,3,2,0:T(4,128)S(1)} %collective-permute-done.2, f32[24,4,10,8,128]{4,1,3,2,0:T(4,128)} %copy-done.9, f32[24,4,10,1,128]{4,1,3,2,0:T(4,128)S(1)} %collective-permute-done.3), kind=kLoop, calls=%fused_computation.10 | loop fusion | flops 9984000 | bytes 9907200 | tf_op jit(solution)/shard_map/concatenate | solution.py:19
  52.3 13.3 %fusion.94 = (f32[4,8,8,128]{3,0,2,1:T(4,128)S(1)}, f32[24,4,8,8,128]{4,1,3,2,0:T(4,128)S(1)}) fusion(f32[24,4,8,8,128]{4,1,3,2,0:T(4,128)S(1)} %copy-done.12, f32[128]{0:T(128)S(1)} %compare_convert_fusion, f32[24,8,8]{2,1,0:T(8,128)S(1)} %copy.85, f32[4,4]{1,0:T(4,128)S(1)} %copy-done, f32[24,4,10,10,130]{4,1,3,2,0:T(4,128)S(1)} %select_maximum_fusion, ...), kind=kOutput, calls=%fused_computation.155 | convolution fusion | flops 55017472 | bytes 21662208 | tf_op jit(solution)/shard_map/fg,mgxyz->mfxyz/dot_general | solution.py:31
  67.7 4.6 copy.97
  72.3 16.4 %gather_fusion = f32[4096,24]{1,0:T(8,128)} fusion(f32[24,8192]{0,1:T(8,128)} %bitcast.91, s32[4096]{0:T(1024)S(1)} %fusion.79), kind=kCustom, calls=%fused_computation.clone | custom fusion | bytes 802816 | tf_op jit(solution)/shard_map/jit(_take)/gather | solution.py:82
  88.7 6.0 bitcast_select_fusion.3
  95.0 148.2 %all-reduce.6.cloned.1.call-done = f32[24,4096]{0,1:T(8,128)} async-done(((f32[24,4096]{0,1:T(8,128)}), f32[24,4096]{0,1:T(8,128)}) %all-reduce.6.cloned.1.call-update) | async-done | bytes 393232 | tf_op jit(solution)/shard_map/psum | solution.py:86
  245.4 2.5 multiply_reduce_fusion.3
  248.9 8.3 %fusion.41 = f32[24,24]{1,0:T(8,128)S(1)} fusion(f32[24,4096]{0,1:T(8,128)} %all-reduce.6.cloned.1.call-done, f32[4096]{0:T(1024)S(1)} %bitcast.120, f32[4096]{0:T(1024)S(1)} %bitcast.119, f32[4096]{0:T(1024)S(1)} %mul.121, f32[4096]{0:T(1024)S(1)} %broadcast_multiply_fusion.10), kind=kOutput, calls=%fused_computation.70 | convolution fusion | flops 28803648 | bytes 461056 | tf_op jit(solution)/shard_map/dot_general | solution.py:89
  257.2 6.3 fusion.95
  265.3 2.6 copy.91
  267.9 13.0 %gather_fusion.1 = f32[4096,24]{1,0:T(8,128)S(1)} fusion(f32[24,8192]{0,1:T(8,128)} %bitcast.92, s32[4096]{0:T(1024)S(1)} %fusion.80), kind=kCustom, calls=%fused_computation.1.clone | custom fusion | bytes 802816 | tf_op jit(solution)/shard_map/jit(_take)/gather | solution.py:82
  280.9 2.7 bitcast_select_fusion.2
  285.0 131.4 %all-reduce.8.cloned.1.call-done = f32[24,4096]{0,1:T(8,128)} async-done(((f32[24,4096]{0,1:T(8,128)}), f32[24,4096]{0,1:T(8,128)}) %all-reduce.8.cloned.1.call-update) | async-done | bytes 393232 | tf_op jit(solution)/shard_map/psum | solution.py:86
  421.1 6.2 fusion.46
  427.4 3.4 fusion.96
  432.3 3.6 copy.92
  435.8 16.4 %gather_fusion.2 = f32[4096,24]{1,0:T(8,128)} fusion(f32[24,8192]{0,1:T(8,128)} %bitcast.93, s32[4096]{0:T(1024)S(1)} %fusion.81), kind=kCustom, calls=%fused_computation.2.clone | custom fusion | bytes 802816 | tf_op jit(solution)/shard_map/jit(_take)/gather | solution.py:82
  452.2 6.0 bitcast_select_fusion.1
  458.7 132.3 %all-reduce.10.cloned.1.call-done = f32[24,4096]{0,1:T(8,128)} async-done(((f32[24,4096]{0,1:T(8,128)}), f32[24,4096]{0,1:T(8,128)}) %all-reduce.10.cloned.1.call-update) | async-done | bytes 393232 | tf_op jit(solution)/shard_map/psum | solution.py:86
  596.7 8.3 %fusion.51 = f32[24,24]{1,0:T(8,128)S(1)} fusion(f32[24,4096]{0,1:T(8,128)} %all-reduce.10.cloned.1.call-done, f32[4096]{0:T(1024)S(1)} %bitcast.124, f32[4096]{0:T(1024)S(1)} %bitcast.123, f32[4096]{0:T(1024)} %mul.131, f32[4096]{0:T(1024)S(1)} %broadcast_multiply_fusion.8), kind=kOutput, calls=%fused_computation.72 | convolution fusion | flops 28803648 | bytes 461056 | tf_op jit(solution)/shard_map/dot_general | solution.py:89
  605.1 3.4 fusion.97
  610.2 2.6 copy.93
  612.8 13.0 %gather_fusion.3 = f32[4096,24]{1,0:T(8,128)S(1)} fusion(f32[24,8192]{0,1:T(8,128)} %bitcast.94, s32[4096]{0:T(1024)S(1)} %fusion.82), kind=kCustom, calls=%fused_computation.3.clone | custom fusion | bytes 802816 | tf_op jit(solution)/shard_map/jit(_take)/gather | solution.py:82
  625.8 2.7 bitcast_select_fusion
  628.7 132.5 %all-reduce.12.cloned.1.call-done = f32[24,4096]{0,1:T(8,128)} async-done(((f32[24,4096]{0,1:T(8,128)}), f32[24,4096]{0,1:T(8,128)}) %all-reduce.12.cloned.1.call-update) | async-done | bytes 393232 | tf_op jit(solution)/shard_map/psum | solution.py:86
  766.0 8.5 %fusion.56 = f32[24,24]{1,0:T(8,128)S(1)} fusion(f32[24,4096]{0,1:T(8,128)} %all-reduce.12.cloned.1.call-done, f32[4096]{0:T(1024)S(1)} %bitcast.126, f32[4096]{0:T(1024)S(1)} %bitcast.125, f32[4096]{0:T(1024)S(1)} %copy-done.20, f32[4096]{0:T(1024)S(1)} %broadcast_multiply_fusion.7), kind=kOutput, calls=%fused_computation.73 | convolution fusion | flops 28803648 | bytes 461056 | tf_op jit(solution)/shard_map/dot_general | solution.py:89
  775.4 3.1 fusion.34
  (140 shorter events, 47.2 us)
Async XLA Ops:
  7.2 45.1 %copy-start = (f32[4,4]{1,0:T(4,128)S(1)}, f32[4,4]{1,0:T(4,128)}, u32[]{:S(2)}) copy-start(f32[4,4]{1,0:T(4,128)} %param.12) | copy-start | bytes 196
  7.2 14.9 %copy-start.6 = (f32[24,4,8,8,128]{4,3,2,1,0:T(8,128)S(1)}, f32[24,4,8,8,128]{4,3,2,1,0:T(8,128)}, u32[]{:S(2)}) copy-start(f32[24,4,8,8,128]{4,3,2,1,0:T(8,128)} %param.10) | copy-start | bytes 9437188
  7.2 11.6 %copy-start.15 = (s32[4,4096]{1,0:T(4,128)S(1)}, s32[4,4096]{1,0:T(4,128)}, u32[]{:S(2)}) copy-start(s32[4,4096]{1,0:T(4,128)} %param.14) | copy-start | bytes 196612
  7.2 11.7 %copy-start.13 = (f32[24,8,8]{0,2,1:T(8,128)S(1)}, f32[24,8,8]{0,2,1:T(8,128)}, u32[]{:S(2)}) copy-start(f32[24,8,8]{0,2,1:T(8,128)} %param.11) | copy-start | bytes 18436
  7.2 13.0 %copy-start.28 = (s32[4,1,1,64]{3,2,1,0:T(1,128)S(1)}, s32[4,1,1,64]{3,2,1,0:T(1,128)}, u32[]{:S(2)}) copy-start(s32[4,1,1,64]{3,2,1,0:T(1,128)} %param.17) | copy-start | bytes 3076
  7.2 13.0 %copy-start.14 = (s32[4,4096]{1,0:T(4,128)S(1)}, s32[4,4096]{1,0:T(4,128)}, u32[]{:S(2)}) copy-start(s32[4,4096]{1,0:T(4,128)} %param.13) | copy-start | bytes 196612
  7.2 236.0 %all-reduce.6.cloned.1.call-start = ((), (), s32[]{:S(2)}) async-start(), calls=%async_computation | async-start | bytes 4194304 | tf_op jit(solution)/shard_map/psum | solution.py:86
  14.4 6.6 collective-permute-start.1
  17.5 7.3 collective-permute-start
  27.9 13.4 %collective-permute-start.2 = (f32[24,4,10,1,128]{4,1,3,2,0:T(4,128)S(1)}, f32[24,4,10,1,128]{4,1,3,2,0:T(4,128)S(1)}, u32[]{:S(2)}, u32[]{:S(2)}) collective-permute-start(f32[24,4,10,1,128]{4,1,3,2,0:T(4,128)S(1)} %get-tuple-element.10), channel_id=1, source_target_pairs={{1,0},{2,1},{3,2},{5,4},{6,5},{7,6},{9,8},{10,9},{11,10},{13,12},{... | collective-permute-start | bytes 1474568 | tf_op jit(solution)/shard_map/ppermute | solution.py:18
  29.2 13.9 %collective-permute-start.3 = (f32[24,4,10,1,128]{4,1,3,2,0:T(4,128)S(1)}, f32[24,4,10,1,128]{4,1,3,2,0:T(4,128)S(1)}, u32[]{:S(2)}, u32[]{:S(2)}) collective-permute-start(f32[24,4,10,1,128]{4,1,3,2,0:T(4,128)S(1)} %get-tuple-element.9), channel_id=1, source_target_pairs={{0,1},{1,2},{2,3},{4,5},{5,6},{6,7},{8,9},{9,10},{10,11},{12,13},{... | collective-permute-start | bytes 1474568 | tf_op jit(solution)/shard_map/ppermute | solution.py:15
  37.4 14.9 %copy-start.10 = (f32[24,4,10,8,128]{4,1,3,2,0:T(4,128)S(1)}, f32[24,4,10,8,128]{4,1,3,2,0:T(4,128)}, u32[]{:S(2)}) copy-start(f32[24,4,10,8,128]{4,1,3,2,0:T(4,128)} %copy-done.9) | copy-start | bytes 11796484
  37.4 14.9 %copy-start.12 = (f32[24,4,8,8,128]{4,1,3,2,0:T(4,128)S(1)}, f32[24,4,8,8,128]{4,1,3,2,0:T(4,128)}, u32[]{:S(2)}) copy-start(f32[24,4,8,8,128]{4,1,3,2,0:T(4,128)} %copy-done.11) | copy-start | bytes 9437188
  94.6 321.8 %all-reduce.8.cloned.1.call-start = ((), (), s32[]{:S(2)}) async-start(), calls=%async_computation.1 | async-start | bytes 4194304 | tf_op jit(solution)/shard_map/psum | solution.py:86
  257.2 6.3 copy-start.18
  265.3 15.6 %copy-start.26 = (pred[4096]{0:T(1024)(128)(4,1)S(1)}, pred[4096]{0:T(1024)(128)(4,1)}, u32[]{:S(2)}) copy-start(pred[4096]{0:T(1024)(128)(4,1)} %get-tuple-element.6) | copy-start | bytes 12292
  280.9 3.3 copy-start.19
  280.9 3.3 copy-start.27
  283.5 136.6 %copy-start.16 = (f32[4,4096]{1,0:T(4,128)S(1)}, f32[4,4096]{1,0:T(4,128)}, u32[]{:S(2)}) copy-start(f32[4,4096]{1,0:T(4,128)} %param.15) | copy-start | bytes 196612
  283.6 137.5 %copy-start.21 = (f32[4096]{0:T(1024)S(1)}, f32[4096]{0:T(1024)}, u32[]{:S(2)}) copy-start(f32[4096]{0:T(1024)} %mul.126) | copy-start | bytes 49156
  283.6 307.5 %all-reduce.10.cloned.1.call-start = ((), (), s32[]{:S(2)}) async-start(), calls=%async_computation.2 | async-start | bytes 4194304 | tf_op jit(solution)/shard_map/psum | solution.py:86
  416.4 2.4 copy-start.7
  421.1 6.3 copy-start.3
  432.3 19.9 %copy-start.24 = (pred[4096]{0:T(1024)(128)(4,1)S(1)}, pred[4096]{0:T(1024)(128)(4,1)}, u32[]{:S(2)}) copy-start(pred[4096]{0:T(1024)(128)(4,1)} %compare_and_fusion.1) | copy-start | bytes 12292
  432.3 19.9 %copy-start.25 = (pred[4096]{0:T(1024)(128)(4,1)S(1)}, pred[4096]{0:T(1024)(128)(4,1)}, u32[]{:S(2)}) copy-start(pred[4096]{0:T(1024)(128)(4,1)} %get-tuple-element.8) | copy-start | bytes 12292
  452.2 6.3 copy-start.17
  458.2 303.0 %all-reduce.12.cloned.1.call-start = ((), (), s32[]{:S(2)}) async-start(), calls=%async_computation.3 | async-start | bytes 4194304 | tf_op jit(solution)/shard_map/psum | solution.py:86
  610.2 15.6 %copy-start.22 = (pred[4096]{0:T(1024)(128)(4,1)S(1)}, pred[4096]{0:T(1024)(128)(4,1)}, u32[]{:S(2)}) copy-start(pred[4096]{0:T(1024)(128)(4,1)} %compare_and_fusion) | copy-start | bytes 12292
  610.2 15.6 %copy-start.23 = (pred[4096]{0:T(1024)(128)(4,1)S(1)}, pred[4096]{0:T(1024)(128)(4,1)}, u32[]{:S(2)}) copy-start(pred[4096]{0:T(1024)(128)(4,1)} %get-tuple-element.5) | copy-start | bytes 12292
  628.5 137.5 %copy-start.20 = (f32[4096]{0:T(1024)S(1)}, f32[4096]{0:T(1024)}, u32[]{:S(2)}) copy-start(f32[4096]{0:T(1024)} %mul.136) | copy-start | bytes 49156
  765.9 9.4 %copy-start.5 = (f32[24,32768]{1,0:T(8,128)S(1)}, f32[24,32768]{1,0:T(8,128)}, u32[]{:S(2)}) copy-start(f32[24,32768]{1,0:T(8,128)} %copy-done.4) | copy-start | bytes 9437188
  775.4 5.3 copy-start.1
  (5 other events, 9.2 us)
Sparse Core Ops, SparseCore 0:
  94.8 148.4 all-reduce.5
  283.7 132.6 all-reduce.7
  458.4 132.6 all-reduce.9
  628.6 132.6 all-reduce.11
where the time goes:
time: 797 us; the launch traced here: 787 us
  waiting for transfers between devices  550 us (69%)
  local copies, waits for them, and re-layouts  99.2 us (12%)
  matrix products  62.4 us (8%)
  other arithmetic  49.2 us (6%)
  between operations  14.7 us (2%)
  starting transfers between devices  11.6 us (1%)
    psum x4, waiting for transfers between devices, on_device(): values = lax.psum(local_vals, ('gx', 'gy'))  545 us
    gather x4, local copies, waits for them, and re-layouts, on_device(): picked = jnp.take(flat_first, obs_cell[batch], axis=1)  58.7 us
    dot_general x4, matrix products, on_device(): jnp.dot(weighted, gterm.T, precision=lax.Precision.HIGHEST)  31.3 us
    unnamed x66, local copies, waits for them, and re-layouts  18.1 us
    select_n x4, other arithmetic, on_device(): local_vals = jnp.where(owned, picked, 0.0)  17.3 us
    dot_general x4, matrix products, apply_mixing(): jnp.dot(mixing.T, prime, precision=lax.Precision.HIGHEST)  16.2 us
  transfers between devices with their start and end apart: 8, of which 6 were waited for; matrix products, arithmetic and copies ran while one was open for 1% of the time, Pallas kernels for 0%

commit v1 on v0

v1 whole, which is shorter than its diff:
```python
import functools

import jax
import jax.numpy as jnp
from jax import lax
from jax.experimental import pallas as pl
from jax.experimental.pallas import tpu as pltpu
from jax.sharding import PartitionSpec as P

OBS_BLOCK = 64
F32 = jnp.float32
BF16 = jnp.bfloat16
NT = (((1,), (1,)), ((), ()))


def pieces(x):
    high = x.astype(BF16).astype(F32)
    return high, x - high


def stacked_dot(left, right):
    lh, ll = pieces(left)
    rh, rl = pieces(right)
    lhs = jnp.concatenate([lh, lh, ll], axis=1).astype(BF16)
    rhs = jnp.concatenate([rh, rl, rh], axis=0).astype(BF16)
    return jnp.dot(lhs, rhs, preferred_element_type=F32)


def halo(block, axis, dim):
    count = lax.axis_size(axis)
    forward = [(i, i + 1) for i in range(count - 1)]
    backward = [(target, source) for source, target in forward]
    size = block.shape[dim]
    low = lax.ppermute(lax.slice_in_dim(block, size - 1, size, axis=dim), axis, forward)
    high = lax.ppermute(lax.slice_in_dim(block, 0, 1, axis=dim), axis, backward)
    return low, high


def forecast_kernel(matrix_ref, c_ref, xlo_ref, xhi_ref, ylo_ref, yhi_ref, wall_ref, out_ref):
    members, fields, cx, cy, nz = c_ref.shape
    sub = lax.broadcasted_iota(jnp.int32, (cy, nz), 0)
    lane = lax.broadcasted_iota(jnp.int32, (cy, nz), 1)

    def one(m, carry):
        for x in range(cx):
            cells = [c_ref[m, f, x] for f in range(fields)]
            wall = jnp.where(lane == 0, jnp.broadcast_to(wall_ref[m][:, x : x + 1], (cy, nz)), 0.0)
            for f in range(fields):
                c = cells[f]
                before = c_ref[m, f, x - 1] if x > 0 else xlo_ref[m, f]
                after = c_ref[m, f, x + 1] if x < cx - 1 else xhi_ref[m, f]
                lap = before + after
                lap = lap + jnp.where(sub == cy - 1, yhi_ref[m, f, x : x + 1], pltpu.roll(c, cy - 1, 0))
                lap = lap + jnp.where(sub == 0, ylo_ref[m, f, x : x + 1], pltpu.roll(c, 1, 0))
                lap = lap + jnp.where(lane == nz - 1, 0.0, pltpu.roll(c, nz - 1, 1))
                lap = lap + jnp.where(lane == 0, 0.0, pltpu.roll(c, 1, 1)) - 6.0 * c
                slope = 0.5 * (after - before)
                mixed = matrix_ref[f, 0] * cells[0]
                for g in range(1, fields):
                    mixed = mixed + matrix_ref[f, g] * cells[g]
                out_ref[m, f, x] = c + 0.5 * (0.15 * lap - 0.6 * slope + mixed - wall * c)
        return carry

    lax.fori_loop(0, members, one, 0)


def forecast(c, wall_texture, matrix):
    members, fields, cx, cy, nz = c.shape
    xlo, xhi = halo(c, "gx", 2)
    ylo, yhi = halo(c, "gy", 3)
    vmem = pl.BlockSpec(memory_space=pltpu.VMEM)
    return pl.pallas_call(
        forecast_kernel,
        out_shape=jax.ShapeDtypeStruct(c.shape, F32),
        in_specs=[pl.BlockSpec(memory_space=pltpu.SMEM)] + [vmem] * 6,
        out_specs=vmem,
        compiler_params=pltpu.CompilerParams(vmem_limit_bytes=40 * 2**20),
        name="forecast",
    )(
        matrix,
        c,
        xlo.reshape(members, fields, cy, nz),
        xhi.reshape(members, fields, cy, nz),
        ylo.reshape(members, fields, cx, nz),
        yhi.reshape(members, fields, cx, nz),
        wall_texture.transpose(0, 2, 1),
    )


def pick_kernel(nz, field_ref, cell_ref, out_ref, wide_ref):
    members, count = out_ref.shape
    rows = field_ref.shape[0] // members
    cell = cell_ref[0]
    z = lax.rem(cell, nz)
    row = lax.div(cell, nz)
    level = lax.rem(lax.broadcasted_iota(jnp.int32, (2 * nz, count), 0), nz)
    hot = jnp.where(level == z, 1.0, 0.0).astype(BF16)
    wide_ref[...] = jnp.dot(field_ref[...], hot, preferred_element_type=F32)
    total = jnp.zeros((members, count), F32)
    for r in range(rows):
        total = jnp.where(row == r, wide_ref[r * members : (r + 1) * members], total)
    out_ref[...] = total


def pick(first, cells):
    members, rows, nz = first.shape
    batches, obs = cells.shape
    turned = first.transpose(1, 0, 2).reshape(rows * members, nz)
    high = lax.reduce_precision(turned, 8, 7)
    low = (turned - high).astype(BF16)
    high = high.astype(BF16)
    count = min(256, obs)
    return pl.pallas_call(
        functools.partial(pick_kernel, nz),
        grid=(batches, obs // count),
        out_shape=jax.ShapeDtypeStruct((batches, members, obs), F32),
        in_specs=[
            pl.BlockSpec((rows * members, 2 * nz), lambda b, i: (0, 0)),
            pl.BlockSpec((None, 1, count), lambda b, i: (b, 0, i)),
        ],
        out_specs=pl.BlockSpec((None, members, count), lambda b, i: (b, 0, i)),
        scratch_shapes=[pltpu.VMEM((rows * members, count), F32)],
        compiler_params=pltpu.CompilerParams(vmem_limit_bytes=32 * 2**20),
        name="pick",
    )(jnp.concatenate([high, low], axis=1), cells[:, None, :])


def window_kernel(
    axes, y_ref, own_ref, value_ref, var_ref, mask_ref, out_ref, part_ref, send_ref, land_ref, send_sem, land_sem
):
    nx, ny = axes
    n = nx * ny
    batches, members, obs = y_ref.shape
    blocks = obs // OBS_BLOCK
    groups = members // 8
    per = min(4, blocks)
    width = per * OBS_BLOCK
    me = lax.axis_index("gx") * ny + lax.axis_index("gy")

    def coords(t):
        return {"gx": lax.div(t, ny), "gy": lax.rem(t, ny)}

    barrier = pltpu.get_barrier_semaphore()

    def greet(d, carry):
        pl.semaphore_signal(
            barrier, inc=1, device_id=coords(lax.rem(me + d, n)), device_id_type=pl.DeviceIdType.MESH
        )
        return carry

    lax.fori_loop(1, n, greet, 0)
    pl.semaphore_wait(barrier, n - 1)

    block_of = lax.broadcasted_iota(jnp.int32, (8, width), 1) // OBS_BLOCK
    group_of = lax.broadcasted_iota(jnp.int32, (8, 128), 1) // members
    eye = jnp.where(
        lax.broadcasted_iota(jnp.int32, (members, members), 0)
        == lax.broadcasted_iota(jnp.int32, (members, members), 1),
        1.0,
        0.0,
    )

    def one(b, mix):
        for c in range(obs // width):
            at = pl.ds(c * width, width)
            y = stacked_dot(mix, y_ref[b, :, at])
            ybar = jnp.sum(y, axis=0, keepdims=True) / members
            dev = y - ybar
            spread = jnp.sum(dev * dev, axis=0, keepdims=True) / (members - 1.0)
            var = var_ref[b, :, at]
            total = spread + var
            root = jnp.sqrt(total)
            g = (value_ref[b, :, at] - ybar) / total - dev * (1.0 / (root * (jnp.sqrt(var) + root)))
            g = jnp.where(own_ref[b, :, at] > 0, g, 0.0)
            lhs = jnp.concatenate(
                [
                    jnp.where(block_of == j, g[8 * i : 8 * i + 8], 0.0)
                    for i in range(groups)
                    for j in range(per)
                ],
                axis=0,
            )
            rhs = jnp.concatenate([dev] * groups + [jnp.zeros((128 - groups * members, width), F32)], axis=0)
            lh, ll = pieces(lhs)
            rh, rl = pieces(rhs)
            lh, ll, rh, rl = (a.astype(BF16) for a in (lh, ll, rh, rl))
            dot = functools.partial(lax.dot_general, dimension_numbers=NT, preferred_element_type=F32)
            both = dot(lh, rh) + (dot(lh, rl) + dot(ll, rh))
            for j in range(per):
                tile = jnp.zeros((8, 128), F32)
                for i in range(groups):
                    k = (i * per + j) * 8
                    tile = jnp.where(group_of == i, both[k : k + 8], tile)
                part_ref[c * per + j] = tile
        mask = mask_ref[b].astype(F32)
        mask2 = jnp.concatenate([mask, mask], axis=1).astype(BF16)
        for q in range(8):
            high, low = pieces(part_ref[:, q, :])
            send_ref[b, :, q, :] = jnp.dot(
                mask2, jnp.concatenate([high, low], axis=0).astype(BF16), preferred_element_type=F32
            )

        def push(d, carry):
            to = lax.rem(me + d, n)
            pltpu.make_async_remote_copy(
                src_ref=send_ref.at[b, to],
                dst_ref=land_ref.at[b, d - 1],
                send_sem=send_sem.at[b],
                recv_sem=land_sem.at[b],
                device_id=coords(to),
                device_id_type=pl.DeviceIdType.MESH,
            ).start()
            return carry

        lax.fori_loop(1, n, push, 0)
        pltpu.make_async_copy(land_ref.at[b], land_ref.at[b], land_sem.at[b]).wait()
        zsum = send_ref[b, me] + jnp.sum(land_ref[b], axis=0)
        zt = jnp.concatenate(
            [(zsum if i == 0 else pltpu.roll(zsum, 128 - i * members, 1))[:, :members] for i in range(groups)],
            axis=0,
        ) / (members - 1.0)
        zt = zt - jnp.mean(zt, axis=1, keepdims=True)
        pltpu.make_async_copy(land_ref.at[b], land_ref.at[b], send_sem.at[b]).wait()
        return mix + stacked_dot(zt, mix)

    out_ref[...] = lax.fori_loop(0, batches, one, eye)


def window(axes, y, own, value, var, masks):
    n = axes[0] * axes[1]
    batches, members, obs = y.shape
    vmem = pl.BlockSpec(memory_space=pltpu.VMEM)
    return pl.pallas_call(
        functools.partial(window_kernel, axes),
        out_shape=jax.ShapeDtypeStruct((members, members), F32),
        in_specs=[vmem] * 5,
        out_specs=vmem,
        scratch_shapes=[
            pltpu.VMEM((obs // OBS_BLOCK, 8, 128), F32),
            pltpu.VMEM((batches, n, 8, 128), F32),
            pltpu.VMEM((batches, n - 1, 8, 128), F32),
            pltpu.SemaphoreType.DMA((batches,)),
            pltpu.SemaphoreType.DMA((batches,)),
        ],
        compiler_params=pltpu.CompilerParams(
            collective_id=0, has_side_effects=True, vmem_limit_bytes=40 * 2**20
        ),
        name="window",
    )(y, own[:, None], value[:, None], var[:, None], masks)


def apply_kernel(mix_ref, state_ref, rough_ref, out_ref, rough_out_ref):
    members, fields, cx, cy, nz = state_ref.shape
    mix = mix_ref[...]
    rough_out_ref[...] = stacked_dot(mix, rough_ref[...])
    for x in range(cx):
        for y in range(cy):
            out_ref[:, 0, x, y, :] = stacked_dot(mix, state_ref[:, 0, x, y, :])


def apply(mix, state, rough):
    members, fields, cx, cy, nz = state.shape
    block = pl.BlockSpec((members, 1, cx, cy, nz), lambda f: (0, f, 0, 0, 0))
    flat = rough.reshape(members, cx * cy)
    state, flat = pl.pallas_call(
        apply_kernel,
        grid=(fields,),
        out_shape=(
            jax.ShapeDtypeStruct(state.shape, F32),
            jax.ShapeDtypeStruct(flat.shape, F32),
        ),
        in_specs=[
            pl.BlockSpec((members, members), lambda f: (0, 0)),
            block,
            pl.BlockSpec((members, cx * cy), lambda f: (0, 0)),
        ],
        out_specs=(block, pl.BlockSpec((members, cx * cy), lambda f: (0, 0))),
        compiler_params=pltpu.CompilerParams(vmem_limit_bytes=32 * 2**20),
        name="apply",
    )(mix, state, flat)
    return state, flat.reshape(rough.shape)


def on_device(
    axes,
    member_flows,
    wall_texture,
    cross_link_matrix,
    obs_owner,
    obs_cell,
    obs_value,
    obs_var,
    local_mask,
):
    members, fields, cx, cy, nz = member_flows.shape
    mytile = lax.axis_index("gx") * axes[1] + lax.axis_index("gy")
    masks = lax.all_gather(local_mask[:, 0, 0], ("gx", "gy"), axis=1)
    own = (obs_owner == mytile).astype(jnp.int32)
    state = forecast(member_flows, wall_texture, cross_link_matrix)
    y = pick(state[:, 0].reshape(members, cx * cy, nz), obs_cell)
    mix = window(axes, y, own, obs_value, obs_var, masks)
    return apply(mix, state, wall_texture)


def solution(mesh):
    axes = (mesh.shape["gx"], mesh.shape["gy"])
    return jax.shard_map(
        functools.partial(on_device, axes),
        mesh=mesh,
        in_specs=(
            P(None, None, "gx", "gy", None),
            P(None, "gx", "gy"),
            P(),
            P(),
            P(),
            P(),
            P(),
            P(None, "gx", "gy", None),
        ),
        out_specs=(P(None, None, "gx", "gy", None), P(None, "gx", "gy")),
        check_vma=False,
    )
```

time: 797 us -> 176 us (0.22); the launches traced: 787 us -> 176 us
  waiting for transfers between devices: 550 us -> 0.01 us
  local copies, waits for them, and re-layouts: 99.2 us -> 8.4 us
  Pallas kernels: 0 us -> 78.8 us
  blocking collectives: 0 us -> 74.5 us
  matrix products: 62.4 us -> 0 us
  other arithmetic: 49.2 us -> 1.07 us
  between operations: 14.7 us -> 0.88 us
    psum x4 -> x0, waiting for transfers between devices: 545 us -> none  [on_device(): values = lax.psum(local_vals, ('gx', 'gy'))]
    pallas_call x0 -> x4, Pallas kernels: none -> 78.8 us  [the longest x1 35.7 us: window(): pl.pallas_call(functools.partial(window_kernel, axes), out_shape=jax.Shap...]
    all_gather x0 -> x1, blocking collectives: none -> 74.5 us  [on_device(): masks = lax.all_gather(local_mask[:, 0, 0], ('gx', 'gy'), axis=1)]
    dot_general x13 -> x0, matrix products: 62.4 us -> none  [the longest x4 31.3 us: on_device(): jnp.dot(weighted, gterm.T, precision=lax.Precision.HIGHEST)]
    gather x4 -> x0, local copies, waits for them, and re-layouts: 58.7 us -> none  [on_device(): picked = jnp.take(flat_first, obs_cell[batch], axis=1)]
    select_n x4 -> x0, other arithmetic: 17.3 us -> none  [on_device(): local_vals = jnp.where(owned, picked, 0.0)]
    reduce_sum x9 -> x0, other arithmetic: 16.8 us -> none  [the longest x4 9.09 us: observation_terms(): ybar = jnp.mean(values, axis=0)]
    unnamed x66 -> x14, local copies, waits for them, and re-layouts: 18.1 us -> 2.33 us
  transfers between devices with their start and end apart: 8 -> 4, of which waited for: 6 -> 0; matrix products, arithmetic and copies ran while one was open for 1% -> 3% of each run, Pallas kernels for 0% -> 0%
where the time goes in v1:
time: 176 us
  Pallas kernels  78.8 us (45%)
  blocking collectives  74.5 us (42%)
  starting transfers between devices  11.9 us (7%)
  local copies, waits for them, and re-layouts  8.4 us (5%)
    all_gather x1, blocking collectives, on_device(): masks = lax.all_gather(local_mask[:, 0, 0], ('gx', 'gy'), axis=1)  74.5 us
    pallas_call x1, Pallas kernels, window(): pl.pallas_call(functools.partial(window_kernel, axes), out_shape=jax.Shap...  35.7 us
    pallas_call x1, Pallas kernels, pick(): pl.pallas_call(functools.partial(pick_kernel, nz), grid=(batches, obs //...  29.1 us
    ppermute x2, starting transfers between devices, halo(): lax.ppermute(lax.slice_in_dim(block, size - 1, size, axis=dim), axis, for...  9.39 us
    pallas_call x1, Pallas kernels, apply(): pl.pallas_call(apply_kernel, grid=(fields,), out_shape=(jax.ShapeDtypeStr...  8.6 us
    pallas_call x1, Pallas kernels, forecast(): pl.pallas_call(forecast_kernel, out_shape=jax.ShapeDtypeStruct(c.shape, F...  5.32 us
    slice x1, local copies, waits for them, and re-layouts, halo(): high = lax.ppermute(lax.slice_in_dim(block, 0, 1, axis=dim), axis, backward)  4.58 us
  transfers between devices with their start and end apart: 4, of which 0 were waited for; matrix products, arithmetic and copies ran while one was open for 3% of the time, Pallas kernels for 0%

profile of v1, /device:TPU:0, one launch (start us, length us, event | category | flops | bytes accessed | tf_op | source)
XLA Modules:
  0.0 175.6 jit_solution(14025958276597843780)
XLA Ops:
  0.6 0.0 copy-start
  0.6 0.0 copy-start.2
  0.7 0.0 copy-start.3
  0.7 0.0 copy-start.4
  0.7 0.0 copy-start.5
  0.7 0.0 copy-start.1
  0.7 2.2 %slice_bitcast_fusion.1 = (f32[24,4,1,8,128]{4,3,1,0,2:T(8,128)}, f32[24,4,1,8,128]{4,3,1,0,2:T(8,128)}) fusion(f32[24,4,8,8,128]{4,3,2,1,0:T(8,128)} %c_ref.1), kind=kLoop, calls=%fused_computation.5 | loop fusion | bytes 1572864
  2.9 1.3 collective-permute-start.1
  4.2 3.8 %collective-permute-start = (f32[24,4,1,8,128]{4,3,1,0,2:T(8,128)}, f32[24,4,1,8,128]{4,3,1,0,2:T(8,128)}, u32[]{:S(2)}, u32[]{:S(2)}) collective-permute-start(f32[24,4,1,8,128]{4,3,1,0,2:T(8,128)} %get-tuple-element.11), channel_id=1, source_target_pairs={{0,4},{4,8},{8,12},{12,16},{16,20},{20,24},{24,28},{1,5},{5,9},{9,... | collective-permute-start | bytes 1179656 | tf_op jit(solution)/shard_map/ppermute | solution.py:34
  8.0 4.6 %fusion.1 = (f32[24,4,8,1,128]{4,3,2,1,0:T(1,128)}, f32[24,4,8,1,128]{4,3,2,1,0:T(1,128)}) fusion(f32[24,4,8,8,128]{4,3,2,1,0:T(8,128)} %c_ref.1), kind=kLoop, calls=%fused_computation.9 | loop fusion | bytes 1572864 | tf_op jit(solution)/shard_map/slice | solution.py:35
  12.5 5.6 %collective-permute-start.2 = (f32[24,4,8,1,128]{4,2,1,0,3:T(8,128)}, f32[24,4,8,1,128]{4,2,1,0,3:T(8,128)}, u32[]{:S(2)}, u32[]{:S(2)}) collective-permute-start(f32[24,4,8,1,128]{4,2,1,0,3:T(8,128)} %bitcast.15), channel_id=1, source_target_pairs={{0,1},{1,2},{2,3},{4,5},{5,6},{6,7},{8,9},{9,10},{10,11},{12,13},{... | collective-permute-start | bytes 1179656 | tf_op jit(solution)/shard_map/ppermute | solution.py:34
  18.2 1.3 collective-permute-start.3
  19.4 0.9 compare_convert_fusion
  20.3 0.0 copy-done.2
  20.3 0.1 copy.32
  20.4 0.1 copy.36.rough_ref
  20.5 0.1 reshape.32.own_ref
  20.6 0.0 copy-done.3
  20.7 74.5 %all-gather = s32[4,32,1,64]{3,0,2,1:T(4,128)S(1)} all-gather(s32[4,1,1,64]{3,0,2,1:T(4,128)} %bitcast.28), channel_id=2, replica_groups=mesh['gx'=8,'gy'=4] {'gx','gy'}, dimensions={1}, use_global_device_ids=true | all-gather | bytes 33792 | tf_op jit(solution)/shard_map/all_gather | solution.py:297
  95.3 0.0 collective-permute-done.1
  95.3 0.0 collective-permute-done
  95.3 0.0 collective-permute-done.2
  95.3 0.0 collective-permute-done.3
  95.3 5.3 %forecast.1.state_ref = f32[24,4,8,8,128]{4,3,2,1,0:T(8,128)S(1)} custom-call(f32[4,4]{1,0:T(4,128)S(1)} %copy-done.1, f32[24,4,8,8,128]{4,3,2,1,0:T(8,128)S(1)} %copy-done, f32[24,4,8,128]{3,2,1,0:T(8,128)} %bitcast.xlo_ref, f32[24,4,8,128]{3,2,1,0:T(8,128)} %bitcast.1.xhi_ref, f32[24,4,8,128]{3,2,1,0:T(8,128)} %bitcast.2.ylo_ref, ...), custom_call_target="tpu_custom_call" | custom-call | tf_op jit(solution)/shard_map/forecast/pallas_call | solution.py:72
  100.7 0.1 slice_bitcast_fusion
  100.7 0.5 copy.33
  101.2 0.1 reduce-precision_convert_fusion
  101.3 0.1 pad_maximum_fusion.field_ref
  101.4 29.1 %pick.1.y_ref = f32[4,24,4096]{2,1,0:T(8,128)S(1)} custom-call(bf16[1536,256]{1,0:T(8,128)(2,1)S(1)} %pad_maximum_fusion.field_ref, s32[4,1,4096]{2,1,0:T(1,128)S(1)} %broadcast_in_dim.14.cell_ref), custom_call_target="tpu_custom_call" | custom-call | tf_op jit(solution)/shard_map/pick/pallas_call | solution.py:113
  130.6 35.7 %window.1.mix_ref = f32[24,24]{1,0:T(8,128)S(1)} custom-call(f32[4,24,4096]{2,1,0:T(8,128)S(1)} %pick.1.y_ref, s32[4,1,4096]{2,1,0:T(1,128)S(1)} %reshape.32.own_ref, f32[4,1,4096]{2,1,0:T(1,128)S(1)} %broadcast_in_dim.17.value_ref, f32[4,1,4096]{2,1,0:T(1,128)S(1)} %broadcast_in_dim.18.var_ref, s32[4,32,64]{2,1,0:T(8,128)S(1)} %bitcast.25), custom_call_target="tpu_custom_call" | custom-call | tf_op jit(solution)/shard_map/window/pallas_call | solution.py:233
  166.3 8.6 %apply.1 = (f32[24,4,8,8,128]{4,3,2,1,0:T(8,128)}, f32[24,64]{1,0:T(8,128)S(1)}) custom-call(f32[24,24]{1,0:T(8,128)S(1)} %window.1.mix_ref, f32[24,4,8,8,128]{4,3,2,1,0:T(8,128)S(1)} %forecast.1.state_ref, f32[24,64]{1,0:T(8,128)S(1)} %copy.36.rough_ref), custom_call_target="tpu_custom_call" | custom-call | tf_op jit(solution)/shard_map/apply/pallas_call | solution.py:265
  174.9 0.7 copy.37
  (8 shorter events, 0.2 us)
Async XLA Ops:
  0.6 94.7 %copy-start = (f32[24,4,8,8,128]{4,3,2,1,0:T(8,128)S(1)}, f32[24,4,8,8,128]{4,3,2,1,0:T(8,128)}, u32[]{:S(2)}) copy-start(f32[24,4,8,8,128]{4,3,2,1,0:T(8,128)} %c_ref.1) | copy-start | bytes 9437188
  0.6 19.7 %copy-start.2 = (f32[24,8,8]{0,2,1:T(8,128)S(1)}, f32[24,8,8]{0,2,1:T(8,128)}, u32[]{:S(2)}) copy-start(f32[24,8,8]{0,2,1:T(8,128)} %param.9) | copy-start | bytes 18436
  0.7 19.9 %copy-start.3 = (s32[4,4096]{1,0:T(4,128)S(1)}, s32[4,4096]{1,0:T(4,128)}, u32[]{:S(2)}) copy-start(s32[4,4096]{1,0:T(4,128)} %param.12) | copy-start | bytes 196612
  0.7 20.0 %copy-start.4 = (f32[4,4096]{1,0:T(4,128)S(1)}, f32[4,4096]{1,0:T(4,128)}, u32[]{:S(2)}) copy-start(f32[4,4096]{1,0:T(4,128)} %param.13) | copy-start | bytes 196612
  0.7 20.0 %copy-start.5 = (f32[4,4096]{1,0:T(4,128)S(1)}, f32[4,4096]{1,0:T(4,128)}, u32[]{:S(2)}) copy-start(f32[4,4096]{1,0:T(4,128)} %param.14) | copy-start | bytes 196612
  0.7 94.6 %copy-start.1 = (f32[4,4]{1,0:T(4,128)S(1)}, f32[4,4]{1,0:T(4,128)}, u32[]{:S(2)}) copy-start(f32[4,4]{1,0:T(4,128)} %matrix_ref.1) | copy-start | bytes 196
  2.9 92.4 %collective-permute-start.1 = (f32[24,4,1,8,128]{4,3,1,0,2:T(8,128)}, f32[24,4,1,8,128]{4,3,1,0,2:T(8,128)}, u32[]{:S(2)}, u32[]{:S(2)}) collective-permute-start(f32[24,4,1,8,128]{4,3,1,0,2:T(8,128)} %get-tuple-element.10), channel_id=1, source_target_pairs={{4,0},{8,4},{12,8},{16,12},{20,16},{24,20},{28,24},{5,1},{9,5},{13... | collective-permute-start | bytes 1179656 | tf_op jit(solution)/shard_map/ppermute | solution.py:35
  4.2 91.1 %collective-permute-start = (f32[24,4,1,8,128]{4,3,1,0,2:T(8,128)}, f32[24,4,1,8,128]{4,3,1,0,2:T(8,128)}, u32[]{:S(2)}, u32[]{:S(2)}) collective-permute-start(f32[24,4,1,8,128]{4,3,1,0,2:T(8,128)} %get-tuple-element.11), channel_id=1, source_target_pairs={{0,4},{4,8},{8,12},{12,16},{16,20},{20,24},{24,28},{1,5},{5,9},{9,... | collective-permute-start | bytes 1179656 | tf_op jit(solution)/shard_map/ppermute | solution.py:34
  12.5 82.8 %collective-permute-start.2 = (f32[24,4,8,1,128]{4,2,1,0,3:T(8,128)}, f32[24,4,8,1,128]{4,2,1,0,3:T(8,128)}, u32[]{:S(2)}, u32[]{:S(2)}) collective-permute-start(f32[24,4,8,1,128]{4,2,1,0,3:T(8,128)} %bitcast.15), channel_id=1, source_target_pairs={{0,1},{1,2},{2,3},{4,5},{5,6},{6,7},{8,9},{9,10},{10,11},{12,13},{... | collective-permute-start | bytes 1179656 | tf_op jit(solution)/shard_map/ppermute | solution.py:34
  18.2 77.2 %collective-permute-start.3 = (f32[24,4,8,1,128]{4,2,1,0,3:T(8,128)}, f32[24,4,8,1,128]{4,2,1,0,3:T(8,128)}, u32[]{:S(2)}, u32[]{:S(2)}) collective-permute-start(f32[24,4,8,1,128]{4,2,1,0,3:T(8,128)} %bitcast.16), channel_id=1, source_target_pairs={{1,0},{2,1},{3,2},{5,4},{6,5},{7,6},{9,8},{10,9},{11,10},{13,12},{... | collective-permute-start | bytes 1179656 | tf_op jit(solution)/shard_map/ppermute | solution.py:35

commit v2 on v1

--- a/solution.py
+++ b/solution.py
@@ -26,18 +26,52 @@
     return jnp.dot(lhs, rhs, preferred_element_type=F32)
 
 
-def halo(block, axis, dim):
-    count = lax.axis_size(axis)
-    forward = [(i, i + 1) for i in range(count - 1)]
-    backward = [(target, source) for source, target in forward]
-    size = block.shape[dim]
-    low = lax.ppermute(lax.slice_in_dim(block, size - 1, size, axis=dim), axis, forward)
-    high = lax.ppermute(lax.slice_in_dim(block, 0, 1, axis=dim), axis, backward)
-    return low, high
-
-
-def forecast_kernel(matrix_ref, c_ref, xlo_ref, xhi_ref, ylo_ref, yhi_ref, wall_ref, out_ref):
+def forecast_kernel(axes, matrix_ref, c_ref, wall_ref, out_ref, x_ref, y_ref, send_sem, land_sem):
     members, fields, cx, cy, nz = c_ref.shape
+    nx, ny = axes
+    gx, gy = lax.axis_index("gx"), lax.axis_index("gy")
+    sides = (
+        (gx > 0, (gx - 1, gy), c_ref.at[:, :, 0], x_ref.at[1], x_ref.at[0]),
+        (gx < nx - 1, (gx + 1, gy), c_ref.at[:, :, cx - 1], x_ref.at[0], x_ref.at[1]),
+        (gy > 0, (gx, gy - 1), c_ref.at[:, :, :, 0, :], y_ref.at[1], y_ref.at[0]),
+        (gy < ny - 1, (gx, gy + 1), c_ref.at[:, :, :, cy - 1, :], y_ref.at[0], y_ref.at[1]),
+    )
+    barrier = pltpu.get_barrier_semaphore()
+    for there, peer, _, _, _ in sides:
+
+        @pl.when(there)
+        def _():
+            pl.semaphore_signal(barrier, inc=1, device_id=peer, device_id_type=pl.DeviceIdType.MESH)
+
+    pl.semaphore_wait(barrier, sum(side[0].astype(jnp.int32) for side in sides))
+
+    def copy(k):
+        _, peer, src, dst, _ = sides[k]
+        return pltpu.make_async_remote_copy(
+            src_ref=src,
+            dst_ref=dst,
+            send_sem=send_sem.at[k],
+            recv_sem=land_sem.at[k ^ 1],
+            device_id=peer,
+            device_id_type=pl.DeviceIdType.MESH,
+        )
+
+    for k, side in enumerate(sides):
+
+        @pl.when(side[0])
+        def _():
+            copy(k).start()
+
+        @pl.when(jnp.logical_not(side[0]))
+        def _():
+            side[4][...] = jnp.zeros(side[4].shape, F32)
+
+    for k, side in enumerate(sides):
+
+        @pl.when(side[0])
+        def _():
+            pltpu.make_async_copy(side[4], side[4], land_sem.at[k]).wait()
+
     sub = lax.broadcasted_iota(jnp.int32, (cy, nz), 0)
     lane = lax.broadcasted_iota(jnp.int32, (cy, nz), 1)
 
@@ -47,11 +81,11 @@
             wall = jnp.where(lane == 0, jnp.broadcast_to(wall_ref[m][:, x : x + 1], (cy, nz)), 0.0)
             for f in range(fields):
                 c = cells[f]
-                before = c_ref[m, f, x - 1] if x > 0 else xlo_ref[m, f]
-                after = c_ref[m, f, x + 1] if x < cx - 1 else xhi_ref[m, f]
+                before = c_ref[m, f, x - 1] if x > 0 else x_ref[0, m, f]
+                after = c_ref[m, f, x + 1] if x < cx - 1 else x_ref[1, m, f]
                 lap = before + after
-                lap = lap + jnp.where(sub == cy - 1, yhi_ref[m, f, x : x + 1], pltpu.roll(c, cy - 1, 0))
-                lap = lap + jnp.where(sub == 0, ylo_ref[m, f, x : x + 1], pltpu.roll(c, 1, 0))
+                lap = lap + jnp.where(sub == cy - 1, y_ref[1, m, f, x : x + 1], pltpu.roll(c, cy - 1, 0))
+                lap = lap + jnp.where(sub == 0, y_ref[0, m, f, x : x + 1], pltpu.roll(c, 1, 0))
                 lap = lap + jnp.where(lane == nz - 1, 0.0, pltpu.roll(c, nz - 1, 1))
                 lap = lap + jnp.where(lane == 0, 0.0, pltpu.roll(c, 1, 1)) - 6.0 * c
                 slope = 0.5 * (after - before)
@@ -62,29 +96,32 @@
         return carry
 
     lax.fori_loop(0, members, one, 0)
-
-
-def forecast(c, wall_texture, matrix):
+    for k, side in enumerate(sides):
+
+        @pl.when(side[0])
+        def _():
+            copy(k).wait_send()
+
+
+def forecast(axes, c, wall_texture, matrix):
     members, fields, cx, cy, nz = c.shape
-    xlo, xhi = halo(c, "gx", 2)
-    ylo, yhi = halo(c, "gy", 3)
     vmem = pl.BlockSpec(memory_space=pltpu.VMEM)
     return pl.pallas_call(
-        forecast_kernel,
+        functools.partial(forecast_kernel, axes),
         out_shape=jax.ShapeDtypeStruct(c.shape, F32),
-        in_specs=[pl.BlockSpec(memory_space=pltpu.SMEM)] + [vmem] * 6,
+        in_specs=[pl.BlockSpec(memory_space=pltpu.SMEM), vmem, vmem],
         out_specs=vmem,
-        compiler_params=pltpu.CompilerParams(vmem_limit_bytes=40 * 2**20),
+        scratch_shapes=[
+            pltpu.VMEM((2, members, fields, cy, nz), F32),
+            pltpu.VMEM((2, members, fields, cx, nz), F32),
+            pltpu.SemaphoreType.DMA((4,)),
+            pltpu.SemaphoreType.DMA((4,)),
+        ],
+        compiler_params=pltpu.CompilerParams(
+            collective_id=1, has_side_effects=True, vmem_limit_bytes=40 * 2**20
+        ),
         name="forecast",
-    )(
-        matrix,
-        c,
-        xlo.reshape(members, fields, cy, nz),
-        xhi.reshape(members, fields, cy, nz),
-        ylo.reshape(members, fields, cx, nz),
-        yhi.reshape(members, fields, cx, nz),
-        wall_texture.transpose(0, 2, 1),
-    )
+    )(matrix, c, wall_texture.transpose(0, 2, 1))
 
 
 def pick_kernel(nz, field_ref, cell_ref, out_ref, wide_ref):
@@ -109,7 +146,7 @@
     high = lax.reduce_precision(turned, 8, 7)
     low = (turned - high).astype(BF16)
     high = high.astype(BF16)
-    count = min(256, obs)
+    count = min(512, obs)
     return pl.pallas_call(
         functools.partial(pick_kernel, nz),
         grid=(batches, obs // count),
@@ -126,7 +163,8 @@
 
 
 def window_kernel(
-    axes, y_ref, own_ref, value_ref, var_ref, mask_ref, out_ref, part_ref, send_ref, land_ref, send_sem, land_sem
+    axes, y_ref, own_ref, value_ref, var_ref, mask_ref, out_ref, part_ref, send_ref, land_ref,
+    masks_ref, send_sem, land_sem, mask_sem
 ):
     nx, ny = axes
     n = nx * ny
@@ -151,6 +189,19 @@
     lax.fori_loop(1, n, greet, 0)
     pl.semaphore_wait(barrier, n - 1)
 
+    def share(d, carry):
+        pltpu.make_async_remote_copy(
+            src_ref=mask_ref,
+            dst_ref=masks_ref.at[d - 1],
+            send_sem=mask_sem.at[0],
+            recv_sem=mask_sem.at[1],
+            device_id=coords(lax.rem(me + d, n)),
+            device_id_type=pl.DeviceIdType.MESH,
+        ).start()
+        return carry
+
+    lax.fori_loop(1, n, share, 0)
+    masks_ref[n - 1] = mask_ref[...]
     block_of = lax.broadcasted_iota(jnp.int32, (8, width), 1) // OBS_BLOCK
     group_of = lax.broadcasted_iota(jnp.int32, (8, 128), 1) // members
     eye = jnp.where(
@@ -192,7 +243,13 @@
                     k = (i * per + j) * 8
                     tile = jnp.where(group_of == i, both[k : k + 8], tile)
                 part_ref[c * per + j] = tile
-        mask = mask_ref[b].astype(F32)
+
+        @pl.when(b == 0)
+        def _():
+            others = masks_ref.at[pl.ds(0, n - 1)]
+            pltpu.make_async_copy(others, others, mask_sem.at[1]).wait()
+
+        mask = masks_ref[:, b, :blocks]
         mask2 = jnp.concatenate([mask, mask], axis=1).astype(BF16)
         for q in range(8):
             high, low = pieces(part_ref[:, q, :])
@@ -203,7 +260,7 @@
         def push(d, carry):
             to = lax.rem(me + d, n)
             pltpu.make_async_remote_copy(
-                src_ref=send_ref.at[b, to],
+                src_ref=send_ref.at[b, n - 1 - d],
                 dst_ref=land_ref.at[b, d - 1],
                 send_sem=send_sem.at[b],
                 recv_sem=land_sem.at[b],
@@ -214,7 +271,7 @@
 
         lax.fori_loop(1, n, push, 0)
         pltpu.make_async_copy(land_ref.at[b], land_ref.at[b], land_sem.at[b]).wait()
-        zsum = send_ref[b, me] + jnp.sum(land_ref[b], axis=0)
+        zsum = send_ref[b, n - 1] + jnp.sum(land_ref[b], axis=0)
         zt = jnp.concatenate(
             [(zsum if i == 0 else pltpu.roll(zsum, 128 - i * members, 1))[:, :members] for i in range(groups)],
             axis=0,
@@ -224,9 +281,11 @@
         return mix + stacked_dot(zt, mix)
 
     out_ref[...] = lax.fori_loop(0, batches, one, eye)
-
-
-def window(axes, y, own, value, var, masks):
+    others = masks_ref.at[pl.ds(0, n - 1)]
+    pltpu.make_async_copy(others, others, mask_sem.at[0]).wait()
+
+
+def window(axes, y, own, value, var, mask):
     n = axes[0] * axes[1]
     batches, members, obs = y.shape
     vmem = pl.BlockSpec(memory_space=pltpu.VMEM)
@@ -239,14 +298,16 @@
             pltpu.VMEM((obs // OBS_BLOCK, 8, 128), F32),
             pltpu.VMEM((batches, n, 8, 128), F32),
             pltpu.VMEM((batches, n - 1, 8, 128), F32),
+            pltpu.VMEM((n,) + mask.shape, F32),
             pltpu.SemaphoreType.DMA((batches,)),
             pltpu.SemaphoreType.DMA((batches,)),
+            pltpu.SemaphoreType.DMA((2,)),
         ],
         compiler_params=pltpu.CompilerParams(
             collective_id=0, has_side_effects=True, vmem_limit_bytes=40 * 2**20
         ),
         name="window",
-    )(y, own[:, None], value[:, None], var[:, None], masks)
+    )(y, own[:, None], value[:, None], var[:, None], mask)
 
 
 def apply_kernel(mix_ref, state_ref, rough_ref, out_ref, rough_out_ref):
@@ -254,8 +315,11 @@
     mix = mix_ref[...]
     rough_out_ref[...] = stacked_dot(mix, rough_ref[...])
     for x in range(cx):
-        for y in range(cy):
-            out_ref[:, 0, x, y, :] = stacked_dot(mix, state_ref[:, 0, x, y, :])
+        for y in range(0, cy, 2):
+            cells = jnp.concatenate([state_ref[:, 0, x, y, :], state_ref[:, 0, x, y + 1, :]], axis=1)
+            moved = stacked_dot(mix, cells)
+            out_ref[:, 0, x, y, :] = moved[:, :nz]
+            out_ref[:, 0, x, y + 1, :] = moved[:, nz:]
 
 
 def apply(mix, state, rough):
@@ -294,11 +358,12 @@
 ):
     members, fields, cx, cy, nz = member_flows.shape
     mytile = lax.axis_index("gx") * axes[1] + lax.axis_index("gy")
-    masks = lax.all_gather(local_mask[:, 0, 0], ("gx", "gy"), axis=1)
+    mask = local_mask[:, 0, 0].astype(F32)
+    mask = jnp.pad(mask, ((0, -mask.shape[0] % 8), (0, -mask.shape[1] % 128)))
     own = (obs_owner == mytile).astype(jnp.int32)
-    state = forecast(member_flows, wall_texture, cross_link_matrix)
+    state = forecast(axes, member_flows, wall_texture, cross_link_matrix)
     y = pick(state[:, 0].reshape(members, cx * cy, nz), obs_cell)
-    mix = window(axes, y, own, obs_value, obs_var, masks)
+    mix = window(axes, y, own, obs_value, obs_var, mask)
     return apply(mix, state, wall_texture)
 
 

time: 176 us -> 105 us (0.60)
  blocking collectives: 74.5 us -> 0 us
  Pallas kernels: 78.8 us -> 93.5 us
  starting transfers between devices: 11.9 us -> 0 us
    all_gather x1 -> x0, blocking collectives: 74.5 us -> none  [on_device(): masks = lax.all_gather(local_mask[:, 0, 0], ('gx', 'gy'), axis=1)]
    pallas_call x1, Pallas kernels: 35.7 us -> 50 us  [window(): pl.pallas_call(functools.partial(window_kernel, axes), out_shape=jax.Shap...]
    pallas_call x1, Pallas kernels: 5.32 us -> 19.1 us  [forecast(): pl.pallas_call(functools.partial(forecast_kernel, axes), out_shape=jax.Sh...]
    ppermute x4 -> x0, starting transfers between devices: 11.9 us -> none  [the longest x2 9.39 us: halo(): lax.ppermute(lax.slice_in_dim(block, size - 1, size, axis=dim), axis, for...]
    pallas_call x1, Pallas kernels: 29.1 us -> 19.2 us  [pick(): pl.pallas_call(functools.partial(pick_kernel, nz), grid=(batches, obs //...]
    slice x1 -> x0, local copies, waits for them, and re-layouts: 4.58 us -> none  [halo(): high = lax.ppermute(lax.slice_in_dim(block, 0, 1, axis=dim), axis, backward)]
    pallas_call x1, Pallas kernels: 8.6 us -> 5.21 us  [apply(): pl.pallas_call(apply_kernel, grid=(fields,), out_shape=(jax.ShapeDtypeStr...]
  transfers between devices with their start and end apart: 4 -> 0, of which waited for: 0 -> 0; matrix products, arithmetic and copies ran while one was open for 3% -> 0% of each run, Pallas kernels for 0% -> 0%
where the time goes in v2:
time: 105 us; the launch traced here: 104 us
  Pallas kernels  93.5 us (89%)
  local copies, waits for them, and re-layouts  8.18 us (8%)
  other arithmetic  1.76 us (2%)
    pallas_call x1, Pallas kernels, window(): pl.pallas_call(functools.partial(window_kernel, axes), out_shape=jax.Shap...  50 us
    pallas_call x1, Pallas kernels, pick(): pl.pallas_call(functools.partial(pick_kernel, nz), grid=(batches, obs //...  19.2 us
    pallas_call x1, Pallas kernels, forecast(): pl.pallas_call(functools.partial(forecast_kernel, axes), out_shape=jax.Sh...  19.1 us
    pallas_call x1, Pallas kernels, apply(): pl.pallas_call(apply_kernel, grid=(fields,), out_shape=(jax.ShapeDtypeStr...  5.21 us
    unnamed x5, local copies, waits for them, and re-layouts  3.42 us

profile of v2, /device:TPU:0, one launch (start us, length us, event | category | flops | bytes accessed | tf_op | source)
XLA Modules:
  0.0 104.2 jit_solution(17460991989186638876)
XLA Ops:
  0.6 0.7 convert_bitcast_fusion
  1.3 0.8 copy.18.rough_ref
  2.1 0.9 compare_convert_fusion
  3.1 0.9 broadcast_in_dim.14.cell_ref
  4.0 0.9 broadcast_in_dim.17.value_ref
  4.9 0.9 broadcast_in_dim.18.var_ref
  5.7 0.9 copy.15
  6.6 0.0 copy-start
  6.6 1.9 %copy-done = f32[24,4,8,8,128]{4,3,2,1,0:T(8,128)S(1)} copy-done((f32[24,4,8,8,128]{4,3,2,1,0:T(8,128)S(1)}, f32[24,4,8,8,128]{4,3,2,1,0:T(8,128)}, u32[]{:S(2)}) %copy-start) | copy-done | bytes 3145752
  8.5 0.0 copy-start.1
  8.5 0.7 copy-done.1
  9.2 19.1 %forecast.1.state_ref = f32[24,4,8,8,128]{4,3,2,1,0:T(8,128)S(1)} custom-call(f32[4,4]{1,0:T(4,128)S(1)} %copy-done.1, f32[24,4,8,8,128]{4,3,2,1,0:T(8,128)S(1)} %copy-done, f32[24,8,8]{2,1,0:T(8,128)S(1)} %bitcast.13), custom_call_target="tpu_custom_call" | custom-call | tf_op jit(solution)/shard_map/forecast/pallas_call | solution.py:109
  28.3 0.1 slice_bitcast_fusion
  28.4 0.5 copy.16
  28.8 0.1 reduce-precision_convert_fusion
  29.0 0.1 pad_maximum_fusion.field_ref
  29.1 19.2 %pick.1.y_ref = f32[4,24,4096]{2,1,0:T(8,128)S(1)} custom-call(bf16[1536,256]{1,0:T(8,128)(2,1)S(1)} %pad_maximum_fusion.field_ref, s32[4,1,4096]{2,1,0:T(1,128)S(1)} %broadcast_in_dim.14.cell_ref), custom_call_target="tpu_custom_call" | custom-call | tf_op jit(solution)/shard_map/pick/pallas_call | solution.py:150
  48.2 50.0 %window.1.mix_ref = f32[24,24]{1,0:T(8,128)S(1)} custom-call(f32[4,24,4096]{2,1,0:T(8,128)S(1)} %pick.1.y_ref, s32[4,1,4096]{2,1,0:T(1,128)S(1)} %reshape.17.own_ref, f32[4,1,4096]{2,1,0:T(1,128)S(1)} %broadcast_in_dim.17.value_ref, f32[4,1,4096]{2,1,0:T(1,128)S(1)} %broadcast_in_dim.18.var_ref, f32[8,128]{1,0:T(8,128)S(1)} %pad.4.mask_ref), custom_call_target="tpu_custom_call" | custom-call | tf_op jit(solution)/shard_map/window/pallas_call | solution.py:292
  98.3 5.2 %apply.1 = (f32[24,4,8,8,128]{4,3,2,1,0:T(8,128)}, f32[24,64]{1,0:T(8,128)S(1)}) custom-call(f32[24,24]{1,0:T(8,128)S(1)} %window.1.mix_ref, f32[24,4,8,8,128]{4,3,2,1,0:T(8,128)S(1)} %forecast.1.state_ref, f32[24,64]{1,0:T(8,128)S(1)} %copy.18.rough_ref), custom_call_target="tpu_custom_call" | custom-call | tf_op jit(solution)/shard_map/apply/pallas_call | solution.py:329
  103.5 0.7 copy.19
  (2 shorter events, 0.1 us)
Async XLA Ops:
  6.6 1.9 %copy-start = (f32[24,4,8,8,128]{4,3,2,1,0:T(8,128)S(1)}, f32[24,4,8,8,128]{4,3,2,1,0:T(8,128)}, u32[]{:S(2)}) copy-start(f32[24,4,8,8,128]{4,3,2,1,0:T(8,128)} %c_ref.1) | copy-start | bytes 9437188
  8.5 0.7 copy-start.1
